TPU v7x, 32 devices: a whole 2x2x4 slice. The times are simulated.
32 devices in a mesh: dp: 4 (over y, x), row: 2 (over core), col: 4 (over z).
Axes of the slice: x: 2, y: 2, z: 4, core: 2. Of those that a mesh axis runs over, the one named last changes fastest.
Arguments:
- step_count: int32 [1], replicated, may hold values from 2 to 11
- ffn_weight: bfloat16 [4096, 10240], P('row', 'col'), may hold values from -40 to 40
- ffn_grads: float32 [4, 4096, 10240], P('dp', 'row', 'col'), may hold values from -80 to 80
- ffn_rows: float32 [4096], P('row'), may hold values from 0.1 to 12
- ffn_cols: float32 [10240], P('col'), may hold values from 0.1 to 1
- attn_weight: bfloat16 [4096, 4096], P('row', 'col'), may hold values from -40 to 40
- attn_grads: float32 [4, 4096, 4096], P('dp', 'row', 'col'), may hold values from -80 to 80
- attn_rows: float32 [4096], P('row'), may hold values from 0.1 to 12
- attn_cols: float32 [4096], P('col'), may hold values from 0.1 to 1
Outputs:
- ffn_weight_new: float32 [4096, 10240], P('row', 'col')
- ffn_update: float32 [4096, 10240], P('row', 'col')
- ffn_rows_new: float32 [4096], P('row')
- ffn_cols_new: float32 [10240], P('col')
- attn_weight_new: float32 [4096, 4096], P('row', 'col')
- attn_update: float32 [4096, 4096], P('row', 'col')
- attn_rows_new: float32 [4096], P('row')
- attn_cols_new: float32 [4096], P('col')
All inputs are finite; a program needn't handle non-finite values.
Results may differ from a plain program's by a relative error of at most 0.0003.
Values sent between devices are 32-bit elements; how exact they have to be, the bound alone decides.
A program may use at most 320 MiB of HBM per device.

v0:
```python
import jax
import jax.numpy as jnp
from jax import lax
from jax.sharding import PartitionSpec as P


def apply_step(w_tile, factor, update):
    return w_tile.astype(jnp.float32) - factor * update


def body(
    step_count,
    ffn_weight,
    ffn_grads,
    ffn_rows,
    ffn_cols,
    attn_weight,
    attn_grads,
    attn_rows,
    attn_cols,
):
    step_value = step_count[0].astype(jnp.float32)
    decay = 1.0 - step_value ** (-0.8)
    weights = (ffn_weight, attn_weight)
    rows_old = (ffn_rows, attn_rows)
    cols_old = (ffn_cols, attn_cols)
    row_devs = lax.axis_size("row")
    col_devs = lax.axis_size("col")
    widths_in = tuple((w_tile.shape[0] * row_devs for w_tile in weights))
    widths_out = tuple((w_tile.shape[1] * col_devs for w_tile in weights))
    summed = (
        lax.psum_scatter(ffn_grads[0], "dp", scatter_dimension=0, tiled=True),
        lax.psum_scatter(attn_grads[0], "dp", scatter_dimension=0, tiled=True),
    )
    share_rows = summed[0].shape[0]
    offset = lax.axis_index("dp") * share_rows
    owned_tiles = tuple(
        (lax.dynamic_slice_in_dim(w_tile, offset, share_rows, 0) for w_tile in weights)
    )
    squares = tuple((g_part * g_part + 1e-30 for g_part in summed))
    row_sums = lax.psum(tuple((jnp.sum(s_part, axis=1) for s_part in squares)), "col")
    col_part = tuple((jnp.sum(s_part, axis=0) for s_part in squares))
    row_full = lax.all_gather(row_sums, "dp", axis=0, tiled=True)
    col_sums = lax.psum(col_part, ("dp", "row"))
    rows_new = tuple(
        (
            decay * rows_old[index] + (1.0 - decay) * (row_full[index] / widths_out[index])
            for index in range(2)
        )
    )
    cols_new = tuple(
        (
            decay * cols_old[index] + (1.0 - decay) * (col_sums[index] / widths_in[index])
            for index in range(2)
        )
    )
    masses = lax.psum(tuple((jnp.sum(r_tile) for r_tile in rows_new)), "row")
    raw_updates = []
    update_sq = []
    for index in range(2):
        row_own = lax.dynamic_slice_in_dim(rows_new[index], offset, share_rows, 0)
        second = row_own[:, None] * cols_new[index][None, :] / (masses[index] / widths_in[index])
        raw_update = summed[index] / jnp.sqrt(second)
        raw_updates.append(raw_update)
        update_sq.append(jnp.sum(raw_update * raw_update))
    update_tot = lax.psum((update_sq[0], update_sq[1]), ("dp", "row", "col"))
    weight_tot = lax.psum(
        tuple((jnp.sum(jnp.square(w_tile.astype(jnp.float32))) for w_tile in weights)),
        ("row", "col"),
    )
    totals = tuple(update_tot) + tuple(weight_tot)
    clipped = []
    factors = []
    for index in range(2):
        entries = widths_in[index] * widths_out[index]
        update_rms = jnp.sqrt(totals[index] / entries)
        clipped.append(raw_updates[index] / jnp.maximum(1.0, update_rms))
        factors.append(0.01 * jnp.sqrt(totals[2 + index] / entries))
    quarter_new = [
        apply_step(owned_tiles[index], factors[index], clipped[index]) for index in range(2)
    ]
    fresh = (
        lax.all_gather(quarter_new[0], "dp", axis=0, tiled=True),
        lax.all_gather(quarter_new[1], "dp", axis=0, tiled=True),
    )
    clipped = (
        lax.all_gather(clipped[0], "dp", axis=0, tiled=True),
        lax.all_gather(clipped[1], "dp", axis=0, tiled=True),
    )
    return (
        fresh[0],
        clipped[0],
        rows_new[0],
        cols_new[0],
        fresh[1],
        clipped[1],
        rows_new[1],
        cols_new[1],
    )


def solution(mesh):
    in_specs = (
        P(),
        P("row", "col"),
        P("dp", "row", "col"),
        P("row"),
        P("col"),
        P("row", "col"),
        P("dp", "row", "col"),
        P("row"),
        P("col"),
    )
    out_specs = (
        P("row", "col"),
        P("row", "col"),
        P("row"),
        P("col"),
        P("row", "col"),
        P("row", "col"),
        P("row"),
        P("col"),
    )
    return jax.shard_map(body, mesh=mesh, in_specs=in_specs, out_specs=out_specs, check_vma=False)
```

profile of v0, /device:TPU:0, one launch (start us, length us, event | category | flops | bytes accessed | tf_op | source)
XLA Modules:
  0.0 1013.2 jit_solution(17527655425020090493)
XLA Ops:
  7.2 0.0 reduce-scatter.5.cloned.1.call-start
  7.2 0.7 reduce-scatter.5.cloned.1.call-update
  7.9 0.0 reduce-scatter.3.cloned.1.call-start
  7.9 0.7 reduce-scatter.3.cloned.1.call-update
  8.7 0.0 all-gather.11.cloned.1.call-start
  8.7 0.0 copy-start.3
  8.7 10.1 multiply_reduce_fusion
  18.8 0.0 copy-done.3
  18.8 0.0 copy-start.8
  18.9 2.8 multiply_reduce_fusion.1
  21.6 19.1 %all-reduce.1 = (f32[]{:T(128)}, f32[]{:T(128)}) all-reduce(f32[]{:T(128)} %multiply_reduce_fusion, f32[]{:T(128)} %multiply_reduce_fusion.1), channel_id=1, replica_groups=mesh['dp'=4,'row'=2,'col'=4] {'row','col'}, use_global_device_ids=true, to_apply=%region_1.0 | all-reduce | flops 2 | bytes 16 | tf_op jit(solution)/shard_map/psum | solution.py:67
  42.2 58.1 %reduce-scatter.5.cloned.1.call-done = f32[512,1024]{1,0:T(8,128)} async-done(((f32[2048,1024]{1,0:T(8,128)}), f32[512,1024]{1,0:T(8,128)}) %reduce-scatter.5.cloned.1.call-update) | async-done | bytes 2097168 | tf_op jit(solution)/shard_map/reduce_scatter | solution.py:33
  100.2 2.1 fusion.2
  102.4 189.1 %reduce-scatter.3.cloned.1.call-done = f32[512,2560]{1,0:T(8,128)} async-done(((f32[2048,2560]{1,0:T(8,128)}), f32[512,2560]{1,0:T(8,128)}) %reduce-scatter.3.cloned.1.call-update) | async-done | bytes 5242896 | tf_op jit(solution)/shard_map/reduce_scatter | solution.py:32
  291.4 3.4 fusion
  294.9 11.7 %all-reduce.3 = (f32[512]{0:T(512)S(1)}, f32[512]{0:T(512)S(1)}) all-reduce(f32[512]{0:T(512)S(1)} %get-tuple-element.9, f32[512]{0:T(512)S(1)} %get-tuple-element.11), channel_id=1, replica_groups=mesh['dp'=4,'row'=2,'col'=4] {'col'}, use_global_device_ids=true, to_apply=%region_4.0 | all-reduce | flops 1024 | bytes 8192 | tf_op jit(solution)/shard_map/psum | solution.py:41
  306.5 7.9 all-gather.1
  314.5 7.2 all-gather
  321.7 0.6 fusion.4
  322.3 3.1 all-reduce.4
  326.7 0.1 dynamic_slice.15
  326.8 0.1 dynamic_slice.13
  326.9 23.4 %all-reduce.2 = (f32[2560]{0:T(1024)S(1)}, f32[1024]{0:T(1024)S(1)}) all-reduce(f32[2560]{0:T(1024)S(1)} %get-tuple-element.8, f32[1024]{0:T(1024)S(1)} %get-tuple-element.10), channel_id=1, replica_groups=mesh['dp'=4,'row'=2,'col'=4] {'dp','row'}, use_global_device_ids=true, to_apply=%region_6.0 | all-reduce | flops 3584 | bytes 28672 | tf_op jit(solution)/shard_map/psum | solution.py:44
  350.2 0.0 copy-done.11
  350.3 0.0 copy-start.4
  350.3 1.5 multiply_reduce_fusion.3
  351.8 4.5 multiply_reduce_fusion.2
  356.3 37.1 %all-reduce = (f32[]{:T(128)}, f32[]{:T(128)}) all-reduce(f32[]{:T(128)} %multiply_reduce_fusion.2, f32[]{:T(128)} %multiply_reduce_fusion.3), channel_id=1, replica_groups=mesh['dp'=4,'row'=2,'col'=4] {'dp','row','col'}, use_global_device_ids=true, to_apply=%region_10.0 | all-reduce | flops 2 | bytes 16 | tf_op jit(solution)/shard_map/psum | solution.py:66
  394.1 3.9 multiply_subtract_fusion.1
  398.0 0.0 copy-done.6
  398.0 0.0 all-gather.11.cloned.1.call-update
  398.0 0.0 all-gather.13.cloned.1.call-start
  398.1 0.5 all-gather.13.cloned.1.call-update
  398.6 0.0 all-gather.7.cloned.1.call-start
  400.1 7.2 multiply_subtract_fusion
  407.3 0.0 all-gather.7.cloned.1.call-update
  407.3 0.0 all-gather.9.cloned.1.call-start
  407.3 0.5 all-gather.9.cloned.1.call-update
  407.9 79.4 %all-gather.11.cloned.1.call-done = f32[2048,1024]{1,0:T(8,128)} async-done(((f32[512,1024]{1,0:T(8,128)}), f32[2048,1024]{1,0:T(8,128)}) %all-gather.11.cloned.1.call-update) | async-done | bytes 8388624 | tf_op jit(solution)/shard_map/all_gather | solution.py:84
  487.3 89.9 %all-gather.13.cloned.1.call-done = f32[2048,1024]{1,0:T(8,128)} async-done(((f32[512,1024]{1,0:T(8,128)}), f32[2048,1024]{1,0:T(8,128)}) %all-gather.13.cloned.1.call-update) | async-done | bytes 8388624 | tf_op jit(solution)/shard_map/all_gather | solution.py:88
  577.2 195.5 %all-gather.7.cloned.1.call-done = f32[2048,2560]{1,0:T(8,128)} async-done(((f32[512,2560]{1,0:T(8,128)}), f32[2048,2560]{1,0:T(8,128)}) %all-gather.7.cloned.1.call-update) | async-done | bytes 20971536 | tf_op jit(solution)/shard_map/all_gather | solution.py:83
  772.7 195.5 %all-gather.9.cloned.1.call-done = f32[2048,2560]{1,0:T(8,128)} async-done(((f32[512,2560]{1,0:T(8,128)}), f32[2048,2560]{1,0:T(8,128)}) %all-gather.9.cloned.1.call-update) | async-done | bytes 20971536 | tf_op jit(solution)/shard_map/all_gather | solution.py:87
  968.2 18.0 %copy.22 = f32[2048,2560]{1,0:T(8,128)} copy(f32[2048,2560]{1,0:T(8,128)} %all-gather.7.cloned.1.call-done) | data formatting | bytes 41943040
  986.2 2.4 copy-done
  988.6 10.6 %copy.23 = f32[2048,2560]{1,0:T(8,128)} copy(f32[2048,2560]{1,0:T(8,128)S(1)} %copy-done) | data formatting | bytes 41943040
  999.3 3.6 copy.24
  1002.9 0.1 slice-done.1
  1003.0 3.4 copy.25
  (25 shorter events, 0.1 us)
Async XLA Ops:
  7.2 93.0 %reduce-scatter.5.cloned.1.call-start = ((), (), s32[]{:S(2)}) async-start(), calls=%async_computation.5 | async-start | bytes 10485760 | tf_op jit(solution)/shard_map/reduce_scatter | solution.py:33
  7.9 283.5 %reduce-scatter.3.cloned.1.call-start = ((), (), s32[]{:S(2)}) async-start(), calls=%async_computation.2 | async-start | bytes 26214400 | tf_op jit(solution)/shard_map/reduce_scatter | solution.py:32
  8.7 478.6 %all-gather.11.cloned.1.call-start = ((), (), s32[]{:S(2)}) async-start(), calls=%async_computation.6 | async-start | bytes 10485760 | tf_op jit(solution)/shard_map/all_gather | solution.py:84
  8.7 10.1 %copy-start.3 = (bf16[2048,1024]{1,0:T(8,128)(2,1)S(1)}, bf16[2048,1024]{1,0:T(8,128)(2,1)}, u32[]{:S(2)}) copy-start(bf16[2048,1024]{1,0:T(8,128)(2,1)} %param.14) | copy-start | bytes 12582916
  18.8 302.9 %copy-start.9 = (f32[2048]{0:T(1024)S(1)}, f32[2048]{0:T(1024)}, u32[]{:S(2)}) copy-start(f32[2048]{0:T(1024)} %param.16) | copy-start | bytes 24580
  18.8 302.9 %copy-start.10 = (f32[2048]{0:T(1024)S(1)}, f32[2048]{0:T(1024)}, u32[]{:S(2)}) copy-start(f32[2048]{0:T(1024)} %param.12) | copy-start | bytes 24580
  18.8 331.4 %copy-start.11 = (f32[1024]{0:T(1024)S(1)}, f32[1024]{0:T(1024)}, u32[]{:S(2)}) copy-start(f32[1024]{0:T(1024)} %param.17) | copy-start | bytes 12292
  18.8 331.4 %copy-start.8 = (f32[2560]{0:T(1024)S(1)}, f32[2560]{0:T(1024)}, u32[]{:S(2)}) copy-start(f32[2560]{0:T(1024)} %param.13) | copy-start | bytes 30724
  100.2 250.1 %copy-start.1 = (f32[512,1024]{1,0:T(8,128)S(1)}, f32[512,1024]{1,0:T(8,128)}, u32[]{:S(2)}) copy-start(f32[512,1024]{1,0:T(8,128)} %reduce-scatter.5.cloned.1.call-done) | copy-start | bytes 6291460
  322.3 75.7 %copy-start.6 = (f32[2048]{0:T(1024)}, f32[2048]{0:T(1024)S(1)}, u32[]{:S(2)}) copy-start(f32[2048]{0:T(1024)S(1)} %get-tuple-element.46) | copy-start | bytes 24580
  322.3 75.7 %copy-start.7 = (f32[2048]{0:T(1024)}, f32[2048]{0:T(1024)S(1)}, u32[]{:S(2)}) copy-start(f32[2048]{0:T(1024)S(1)} %get-tuple-element.42) | copy-start | bytes 24580
  350.3 47.8 %copy-start.5 = (f32[1024]{0:T(1024)}, f32[1024]{0:T(1024)S(1)}, u32[]{:S(2)}) copy-start(f32[1024]{0:T(1024)S(1)} %multiply_add_fusion.5) | copy-start | bytes 12292
  350.3 49.7 %copy-start.4 = (f32[2560]{0:T(1024)}, f32[2560]{0:T(1024)S(1)}, u32[]{:S(2)}) copy-start(f32[2560]{0:T(1024)S(1)} %multiply_add_fusion.2) | copy-start | bytes 30724
  398.0 179.1 %all-gather.13.cloned.1.call-start = ((), (), s32[]{:S(2)}) async-start(), calls=%async_computation.7 | async-start | bytes 10485760 | tf_op jit(solution)/shard_map/all_gather | solution.py:88
  398.6 374.1 %all-gather.7.cloned.1.call-start = ((), (), s32[]{:S(2)}) async-start(), calls=%async_computation.3 | async-start | bytes 26214400 | tf_op jit(solution)/shard_map/all_gather | solution.py:83
  407.3 560.9 %all-gather.9.cloned.1.call-start = ((), (), s32[]{:S(2)}) async-start(), calls=%async_computation.4 | async-start | bytes 26214400 | tf_op jit(solution)/shard_map/all_gather | solution.py:87
  968.2 20.4 %copy-start = (f32[2048,2560]{1,0:T(8,128)S(1)}, f32[2048,2560]{1,0:T(8,128)}, u32[]{:S(2)}) copy-start(f32[2048,2560]{1,0:T(8,128)} %all-gather.9.cloned.1.call-done) | copy-start | bytes 62914564
  968.2 34.7 %slice-start = ((s8[8388608]{0:T(1024)(128)(4,1)}), s8[4194304]{0:T(1024)(128)(4,1)S(1)}, s32[]{:S(2)}) async-start(s8[8388608]{0:T(1024)(128)(4,1)} %bitcast.9), calls=%async_computation.8 | async-start | bytes 8388608
  988.6 10.6 %copy-start.2 = (f32[2048,1024]{1,0:T(8,128)S(1)}, f32[2048,1024]{1,0:T(8,128)}, u32[]{:S(2)}) copy-start(f32[2048,1024]{1,0:T(8,128)} %all-gather.11.cloned.1.call-done) | copy-start | bytes 25165828
  988.6 14.3 %slice-start.1 = ((s8[8388608]{0:T(1024)(128)(4,1)}), s8[4194304]{0:T(1024)(128)(4,1)S(1)}, s32[]{:S(2)}) async-start(s8[8388608]{0:T(1024)(128)(4,1)} %bitcast.9), calls=%async_computation.9 | async-start | bytes 8388608
Sparse Core Ops, SparseCore 0:
  11.1 89.0 reduce-scatter.4
  103.6 187.7 reduce-scatter.2
  398.2 89.0 all-gather.10
  489.5 87.5 all-gather.12
  579.5 193.1 all-gather.6
  775.0 193.1 all-gather.8
where the time goes:
time: 1010 us
  waiting for transfers between devices  810 us (80%)
  blocking collectives  110 us (11%)
  local copies, waits for them, and re-layouts  38.3 us (4%)
  other arithmetic  36.2 us (4%)
  between operations  19 us (2%)
    all_gather x1, waiting for transfers between devices, body(): lax.all_gather(clipped[0], 'dp', axis=0, tiled=True)  196 us
    all_gather x1, waiting for transfers between devices, body(): lax.all_gather(quarter_new[0], 'dp', axis=0, tiled=True)  196 us
    reduce_scatter x1, waiting for transfers between devices, body(): lax.psum_scatter(ffn_grads[0], 'dp', scatter_dimension=0, tiled=True)  189 us
    all_gather x1, waiting for transfers between devices, body(): lax.all_gather(clipped[1], 'dp', axis=0, tiled=True)  89.9 us
    all_gather x1, waiting for transfers between devices, body(): lax.all_gather(quarter_new[1], 'dp', axis=0, tiled=True)  79.4 us
    reduce_scatter x1, waiting for transfers between devices, body(): lax.psum_scatter(attn_grads[0], 'dp', scatter_dimension=0, tiled=True)  58.1 us
    unnamed x32, local copies, waits for them, and re-layouts  38.2 us
    psum x1, blocking collectives, body(): update_tot = lax.psum((update_sq[0], update_sq[1]), ('dp', 'row', 'col'))  37.1 us
  transfers between devices with their start and end apart: 6, of which 6 were waited for; matrix products, arithmetic and copies ran while one was open for 2% of the time, Pallas kernels for 0%

commit v1 on v0

--- a/solution.py
+++ b/solution.py
@@ -32,11 +32,9 @@
         lax.psum_scatter(ffn_grads[0], "dp", scatter_dimension=0, tiled=True),
         lax.psum_scatter(attn_grads[0], "dp", scatter_dimension=0, tiled=True),
     )
+    whole = tuple(lax.all_gather(g_part, "dp", axis=0, tiled=True) for g_part in summed)
     share_rows = summed[0].shape[0]
     offset = lax.axis_index("dp") * share_rows
-    owned_tiles = tuple(
-        (lax.dynamic_slice_in_dim(w_tile, offset, share_rows, 0) for w_tile in weights)
-    )
     squares = tuple((g_part * g_part + 1e-30 for g_part in summed))
     row_sums = lax.psum(tuple((jnp.sum(s_part, axis=1) for s_part in squares)), "col")
     col_part = tuple((jnp.sum(s_part, axis=0) for s_part in squares))
@@ -70,23 +68,16 @@
     )
     totals = tuple(update_tot) + tuple(weight_tot)
     clipped = []
-    factors = []
+    fresh = []
     for index in range(2):
         entries = widths_in[index] * widths_out[index]
         update_rms = jnp.sqrt(totals[index] / entries)
-        clipped.append(raw_updates[index] / jnp.maximum(1.0, update_rms))
-        factors.append(0.01 * jnp.sqrt(totals[2 + index] / entries))
-    quarter_new = [
-        apply_step(owned_tiles[index], factors[index], clipped[index]) for index in range(2)
-    ]
-    fresh = (
-        lax.all_gather(quarter_new[0], "dp", axis=0, tiled=True),
-        lax.all_gather(quarter_new[1], "dp", axis=0, tiled=True),
-    )
-    clipped = (
-        lax.all_gather(clipped[0], "dp", axis=0, tiled=True),
-        lax.all_gather(clipped[1], "dp", axis=0, tiled=True),
-    )
+        factor = 0.01 * jnp.sqrt(totals[2 + index] / entries)
+        mean = masses[index] / widths_in[index]
+        second = rows_new[index][:, None] * cols_new[index][None, :] / mean
+        update = whole[index] / jnp.sqrt(second) / jnp.maximum(1.0, update_rms)
+        clipped.append(update)
+        fresh.append(apply_step(weights[index], factor, update))
     return (
         fresh[0],
         clipped[0],

time: 1010 us -> 610 us (0.60)
  waiting for transfers between devices: 810 us -> 423 us
  local copies, waits for them, and re-layouts: 38.3 us -> 0.2 us
  other arithmetic: 36.2 us -> 58.7 us
    all_gather x4 -> x2, waiting for transfers between devices: 560 us -> 139 us  [body(): lax.all_gather(g_part, 'dp', axis=0, tiled=True)]
    unnamed x32 -> x20, local copies, waits for them, and re-layouts: 38.2 us -> 0.05 us
    reduce_scatter x1, waiting for transfers between devices: 58.1 us -> 91.5 us  [body(): lax.psum_scatter(attn_grads[0], 'dp', scatter_dimension=0, tiled=True)]
    sub x2, other arithmetic: 11.1 us -> 35.3 us  [apply_step(): return w_tile.astype(jnp.float32) - factor * update]
  transfers between devices with their start and end apart: 6 -> 4, of which waited for: 6 -> 3; matrix products, arithmetic and copies ran while one was open for 2% -> 5% of each run, Pallas kernels for 0% -> 0%
where the time goes in v1:
time: 610 us; the launch traced here: 609 us
  waiting for transfers between devices  423 us (69%)
  blocking collectives  109 us (18%)
  other arithmetic  58.7 us (10%)
  between operations  18.7 us (3%)
    reduce_scatter x1, waiting for transfers between devices, body(): lax.psum_scatter(ffn_grads[0], 'dp', scatter_dimension=0, tiled=True)  191 us
    all_gather x2, waiting for transfers between devices, body(): lax.all_gather(g_part, 'dp', axis=0, tiled=True)  139 us
    reduce_scatter x1, waiting for transfers between devices, body(): lax.psum_scatter(attn_grads[0], 'dp', scatter_dimension=0, tiled=True)  91.5 us
    psum x1, blocking collectives, body(): update_tot = lax.psum((update_sq[0], update_sq[1]), ('dp', 'row', 'col'))  40.1 us
    sub x2, other arithmetic, apply_step(): return w_tile.astype(jnp.float32) - factor * update  35.3 us
    psum x1, blocking collectives, body(): col_sums = lax.psum(col_part, ('dp', 'row'))  24.2 us
    psum x1, blocking collectives, body(): lax.psum(tuple((jnp.sum(jnp.square(w_tile.astype(jnp.float32))) for w_til...  17.4 us
    all_gather x2, blocking collectives, body(): row_full = lax.all_gather(row_sums, 'dp', axis=0, tiled=True)  15.1 us
  transfers between devices with their start and end apart: 4, of which 3 were waited for; matrix products, arithmetic and copies ran while one was open for 5% of the time, Pallas kernels for 0%

profile of v1, /device:TPU:0, one launch (start us, length us, event | category | flops | bytes accessed | tf_op | source)
XLA Modules:
  0.0 609.3 jit_solution(7173546384482473255)
XLA Ops:
  7.2 0.0 reduce-scatter.5.cloned.1.call-start
  7.2 0.7 reduce-scatter.5.cloned.1.call-update
  7.9 0.0 reduce-scatter.3.cloned.1.call-start
  7.9 0.7 reduce-scatter.3.cloned.1.call-update
  8.7 0.0 all-gather.7.cloned.1.call-start
  8.7 91.5 %reduce-scatter.5.cloned.1.call-done = f32[512,1024]{1,0:T(8,128)} async-done(((f32[2048,1024]{1,0:T(8,128)}), f32[512,1024]{1,0:T(8,128)}) %reduce-scatter.5.cloned.1.call-update) | async-done | bytes 2097168 | tf_op jit(solution)/shard_map/reduce_scatter | solution.py:33
  100.2 0.0 all-gather.7.cloned.1.call-update
  100.2 0.0 all-gather.5.cloned.1.call-start
  100.3 191.2 %reduce-scatter.3.cloned.1.call-done = f32[512,2560]{1,0:T(8,128)} async-done(((f32[2048,2560]{1,0:T(8,128)}), f32[512,2560]{1,0:T(8,128)}) %reduce-scatter.3.cloned.1.call-update) | async-done | bytes 5242896 | tf_op jit(solution)/shard_map/reduce_scatter | solution.py:32
  291.4 0.0 all-gather.5.cloned.1.call-update
  291.5 0.0 copy-start.1
  291.5 0.0 copy-start
  291.5 10.1 %fusion = f32[]{:T(128)} fusion(bf16[2048,2560]{1,0:T(8,128)(2,1)} %param.10), kind=kLoop, calls=%fused_computation.2 | loop fusion | flops 15728639 | bytes 10485764 | tf_op jit(solution)/shard_map/reduce_sum | solution.py:66
  301.6 0.0 copy-done.1
  301.6 0.0 copy-start.7
  301.6 0.0 copy-start.8
  301.6 0.0 copy-start.9
  301.6 0.0 copy-start.6
  301.6 2.8 fusion.1
  304.4 17.4 %all-reduce.1 = (f32[]{:T(128)}, f32[]{:T(128)}) all-reduce(f32[]{:T(128)} %fusion, f32[]{:T(128)} %fusion.1), channel_id=1, replica_groups=mesh['dp'=4,'row'=2,'col'=4] {'row','col'}, use_global_device_ids=true, to_apply=%region_1.0 | all-reduce | flops 2 | bytes 16 | tf_op jit(solution)/shard_map/psum | solution.py:65
  323.9 0.0 copy-done
  323.9 0.4 fusion.4
  324.3 3.4 fusion.2
  327.7 8.7 %all-reduce.3 = (f32[512]{0:T(512)S(1)}, f32[512]{0:T(512)S(1)}) all-reduce(f32[512]{0:T(512)S(1)} %get-tuple-element.9, f32[512]{0:T(512)S(1)} %get-tuple-element.11), channel_id=1, replica_groups=mesh['dp'=4,'row'=2,'col'=4] {'col'}, use_global_device_ids=true, to_apply=%region_4.0 | all-reduce | flops 1024 | bytes 8192 | tf_op jit(solution)/shard_map/psum | solution.py:39
  336.4 7.9 %all-gather.1 = f32[4,1,512]{2,1,0:T(1,128)S(1)} all-gather(f32[1,1,512]{2,1,0:T(1,128)S(1)} %bitcast.12), channel_id=1, replica_groups=mesh['dp'=4,'row'=2,'col'=4] {'dp'}, dimensions={0}, use_global_device_ids=true | all-gather | bytes 10240 | tf_op jit(solution)/shard_map/all_gather | solution.py:41
  344.3 7.2 %all-gather = f32[4,1,512]{2,1,0:T(1,128)S(1)} all-gather(f32[1,1,512]{2,1,0:T(1,128)S(1)} %bitcast.11), channel_id=1, replica_groups=mesh['dp'=4,'row'=2,'col'=4] {'dp'}, dimensions={0}, use_global_device_ids=true | all-gather | bytes 10240 | tf_op jit(solution)/shard_map/all_gather | solution.py:41
  351.6 0.0 copy-done.7
  351.6 0.0 copy-done.8
  351.6 0.6 fusion.6
  352.2 0.0 copy-start.4
  352.2 3.1 all-reduce.4
  356.6 0.1 dynamic_slice.7
  356.7 0.1 dynamic_slice.6
  356.8 24.2 %all-reduce.2 = (f32[2560]{0:T(1024)S(1)}, f32[1024]{0:T(1024)S(1)}) all-reduce(f32[2560]{0:T(1024)S(1)} %get-tuple-element.8, f32[1024]{0:T(1024)S(1)} %get-tuple-element.10), channel_id=1, replica_groups=mesh['dp'=4,'row'=2,'col'=4] {'dp','row'}, use_global_device_ids=true, to_apply=%region_6.0 | all-reduce | flops 3584 | bytes 28672 | tf_op jit(solution)/shard_map/psum | solution.py:42
  381.0 0.0 copy-done.9
  381.0 0.0 copy-done.6
  381.0 0.0 copy-start.2
  381.0 1.5 multiply_reduce_fusion.1
  382.5 4.5 multiply_reduce_fusion
  387.1 40.1 %all-reduce = (f32[]{:T(128)}, f32[]{:T(128)}) all-reduce(f32[]{:T(128)} %multiply_reduce_fusion, f32[]{:T(128)} %multiply_reduce_fusion.1), channel_id=1, replica_groups=mesh['dp'=4,'row'=2,'col'=4] {'dp','row','col'}, use_global_device_ids=true, to_apply=%region_10.0 | all-reduce | flops 2 | bytes 16 | tf_op jit(solution)/shard_map/psum | solution.py:64
  428.5 0.0 all-gather.7.cloned.1.call-done
  428.6 9.9 %convert_subtract_fusion.1 = (f32[2048,1024]{1,0:T(8,128)}, f32[2048,1024]{1,0:T(8,128)}) fusion(bf16[2048,1024]{1,0:T(8,128)(2,1)} %param.14, f32[]{:T(128)S(6)} %mul.157, f32[]{:T(128)S(6)} %max.7, f32[2048,1024]{1,0:T(8,128)} %all-gather.7.cloned.1.call-done, f32[]{:T(128)S(6)} %div.88, f32[1024]{0:T(1024)S(1)} %multiply_add_fusion.5, ...), kind=kLoop, calls=%fused_computation.4 | loop fusion | flops 14680064 | bytes 29372428 | tf_op jit(solution)/shard_map/sub | solution.py:8
  438.5 0.0 copy-done.4
  438.5 0.0 copy-done.5
  438.5 138.9 %all-gather.5.cloned.1.call-done = f32[2048,2560]{1,0:T(8,128)} async-done(((f32[512,2560]{1,0:T(8,128)}), f32[2048,2560]{1,0:T(8,128)}) %all-gather.5.cloned.1.call-update) | async-done | bytes 20971536 | tf_op jit(solution)/shard_map/all_gather | solution.py:35
  577.4 0.0 copy-done.3
  577.4 0.0 copy-done.2
  577.4 25.4 %convert_subtract_fusion = (f32[2048,2560]{1,0:T(8,128)}, f32[2048,2560]{1,0:T(8,128)}) fusion(bf16[2048,2560]{1,0:T(8,128)(2,1)} %param.10, f32[]{:T(128)S(6)} %mul.135, f32[]{:T(128)S(6)} %max.6, f32[2048,2560]{1,0:T(8,128)} %all-gather.5.cloned.1.call-done, f32[]{:T(128)S(6)} %div.77, f32[2560]{0:T(1024)S(1)} %multiply_add_fusion.2, ...), kind=kLoop, calls=%fused_computation | loop fusion | flops 36700160 | bytes 73418768 | tf_op jit(solution)/shard_map/sub | solution.py:8
  (6 shorter events, 0.0 us)
Async XLA Ops:
  7.2 93.0 %reduce-scatter.5.cloned.1.call-start = ((), (), s32[]{:S(2)}) async-start(), calls=%async_computation.4 | async-start | bytes 10485760 | tf_op jit(solution)/shard_map/reduce_scatter | solution.py:33
  7.9 283.5 %reduce-scatter.3.cloned.1.call-start = ((), (), s32[]{:S(2)}) async-start(), calls=%async_computation.2 | async-start | bytes 26214400 | tf_op jit(solution)/shard_map/reduce_scatter | solution.py:32
  8.7 419.9 %all-gather.7.cloned.1.call-start = ((), (), s32[]{:S(2)}) async-start(), calls=%async_computation.5 | async-start | bytes 10485760 | tf_op jit(solution)/shard_map/all_gather | solution.py:35
  100.2 477.2 %all-gather.5.cloned.1.call-start = ((), (), s32[]{:S(2)}) async-start(), calls=%async_computation.3 | async-start | bytes 26214400 | tf_op jit(solution)/shard_map/all_gather | solution.py:35
  291.5 10.1 %copy-start.1 = (bf16[2048,1024]{1,0:T(8,128)(2,1)S(1)}, bf16[2048,1024]{1,0:T(8,128)(2,1)}, u32[]{:S(2)}) copy-start(bf16[2048,1024]{1,0:T(8,128)(2,1)} %param.14) | copy-start | bytes 12582916
  291.5 32.4 %copy-start = (f32[512,1024]{1,0:T(8,128)S(1)}, f32[512,1024]{1,0:T(8,128)}, u32[]{:S(2)}) copy-start(f32[512,1024]{1,0:T(8,128)} %reduce-scatter.5.cloned.1.call-done) | copy-start | bytes 6291460
  301.6 50.0 %copy-start.7 = (f32[2048]{0:T(1024)S(1)}, f32[2048]{0:T(1024)}, u32[]{:S(2)}) copy-start(f32[2048]{0:T(1024)} %param.16) | copy-start | bytes 24580
  301.6 50.0 %copy-start.8 = (f32[2048]{0:T(1024)S(1)}, f32[2048]{0:T(1024)}, u32[]{:S(2)}) copy-start(f32[2048]{0:T(1024)} %param.12) | copy-start | bytes 24580
  301.6 79.4 %copy-start.9 = (f32[1024]{0:T(1024)S(1)}, f32[1024]{0:T(1024)}, u32[]{:S(2)}) copy-start(f32[1024]{0:T(1024)} %param.17) | copy-start | bytes 12292
  301.6 79.4 %copy-start.6 = (f32[2560]{0:T(1024)S(1)}, f32[2560]{0:T(1024)}, u32[]{:S(2)}) copy-start(f32[2560]{0:T(1024)} %param.13) | copy-start | bytes 30724
  352.2 86.3 %copy-start.4 = (f32[2048]{0:T(1024)}, f32[2048]{0:T(1024)S(1)}, u32[]{:S(2)}) copy-start(f32[2048]{0:T(1024)S(1)} %get-tuple-element.27) | copy-start | bytes 24580
  352.2 225.2 %copy-start.3 = (f32[2048]{0:T(1024)}, f32[2048]{0:T(1024)S(1)}, u32[]{:S(2)}) copy-start(f32[2048]{0:T(1024)S(1)} %get-tuple-element.31) | copy-start | bytes 24580
  381.0 57.5 %copy-start.5 = (f32[1024]{0:T(1024)}, f32[1024]{0:T(1024)S(1)}, u32[]{:S(2)}) copy-start(f32[1024]{0:T(1024)S(1)} %multiply_add_fusion.5) | copy-start | bytes 12292
  381.0 196.4 %copy-start.2 = (f32[2560]{0:T(1024)}, f32[2560]{0:T(1024)S(1)}, u32[]{:S(2)}) copy-start(f32[2560]{0:T(1024)S(1)} %multiply_add_fusion.2) | copy-start | bytes 30724
Sparse Core Ops, SparseCore 0:
  11.1 89.0 reduce-scatter.4
  103.6 187.7 reduce-scatter.2
  293.3 88.3 all-gather.6
  383.4 193.9 all-gather.4

commit v2 on v1

v2 whole, which is shorter than its diff:
```python
import functools

import jax
import jax.numpy as jnp
from jax import lax
from jax.experimental import pallas as pl
from jax.experimental.pallas import tpu as pltpu
from jax.sharding import PartitionSpec as P

MESH = pl.DeviceIdType.MESH
LANES = 128
STRIP = 8
CUTS = (4, 2)


def gray(index):
    high = index // 2
    return index + high * (5 - 2 * index)


def lane_sums(x):
    total = x[:, :LANES]
    for c in range(1, x.shape[1] // LANES):
        total = total + x[:, c * LANES : (c + 1) * LANES]
    return total


def to_lanes(ref, out_ref, at):
    rows = ref.shape[0]
    for c in range(rows // LANES):
        turned = ref[pl.ds(c * LANES, LANES), :].T
        out_ref[:, pl.ds(at + c * LANES, LANES)] = jnp.sum(turned, axis=0, keepdims=True)


def kernel(
    sizes,
    decay_ref,
    g1, g2, w1, w2, r1, r2, c1, c2,
    full1, full2, rn1, rn2, cn1, cn2, tot,
    rb1, rb2, lb1, lb2, wb1, wb2, ca1, ca2, rp1, rp2, ic1, ic2,
    row_msg, col_msg, upd_msg, end_msg,
    own_row, own_col, own_upd, own_end,
    send_sem, recv_sem, load_sem, keep_sem, w_sem,
    s_row, q_row, s_col, q_col, s_upd, q_upd, s_end, q_end,
):
    dp_n, row_n, col_n = sizes
    grads, fulls, rbs, lbs = (g1, g2), (full1, full2), (rb1, rb2), (lb1, lb2)
    wts, wbs, cas, rps, ics = (w1, w2), (wb1, wb2), (ca1, ca2), (rp1, rp2), (ic1, ic2)
    olds, cols, rns, cns = (r1, r2), (c1, c2), (rn1, rn2), (cn1, cn2)
    tile = g1.shape[0]
    quarter, half = tile // dp_n, tile // (2 * dp_n)
    widths = (g1.shape[1], g2.shape[1])
    steps = dp_n - 1
    dp, row, col = lax.axis_index("dp"), lax.axis_index("row"), lax.axis_index("col")
    pos = gray(dp)
    plane_n = dp_n * row_n
    slot = pos * row_n + row
    subs = [(m, j) for m in range(2) for j in range(CUTS[m])]

    def plane_peer(i):
        other = (slot + i) % plane_n
        return {"dp": gray(other // row_n), "row": other % row_n}

    def col_peer(i):
        return {"col": (col + i) % col_n}

    def block(d, back):
        return (pos + dp_n - back) % dp_n if d == 0 else (pos + back) % dp_n

    def place(m, j, d, at):
        n = half // CUTS[m]
        return pl.ds(pl.multiple_of(at * quarter + d * half + j * n, 8), n)

    def piece(m, j):
        n = half // CUTS[m]
        return pl.ds(j * n, n)

    def load(d, s, k):
        m, j = subs[k]
        return pltpu.make_async_copy(
            grads[m].at[place(m, j, d, block(d, s + 2)), :],
            lbs[m].at[d, s, piece(m, j), :],
            load_sem.at[d, s, k],
        )

    def keep(d, k):
        m, j = subs[k]
        return pltpu.make_async_copy(
            rbs[m].at[d, steps - 1, piece(m, j), :],
            fulls[m].at[place(m, j, d, pos), :],
            keep_sem.at[d, k],
        )

    def send(d, s, k):
        m, j = subs[k]
        if s < steps:
            if s == 0:
                src = grads[m].at[place(m, j, d, block(d, 1)), :]
            else:
                src = rbs[m].at[d, s - 1, piece(m, j), :]
            dst = rbs[m].at[d, s, piece(m, j), :]
        else:
            t = s - steps
            dst = fulls[m].at[place(m, j, d, block(d, t)), :]
            src = rbs[m].at[d, steps - 1, piece(m, j), :] if t == 0 else dst
        to = gray((pos + 1) % dp_n if d == 0 else (pos + dp_n - 1) % dp_n)
        return pltpu.make_async_remote_copy(
            src_ref=src, dst_ref=dst,
            send_sem=send_sem.at[d, s, k], recv_sem=recv_sem.at[d, s, k],
            device_id={"dp": to}, device_id_type=MESH,
        )

    def message(own, inbox, ss, qs, i, peer):
        return pltpu.make_async_remote_copy(
            src_ref=own, dst_ref=inbox.at[i],
            send_sem=ss.at[i], recv_sem=qs.at[i],
            device_id=peer(i), device_id_type=MESH,
        )

    def exchange(own, inbox, ss, qs, n, peer):
        for i in range(1, n):
            message(own, inbox, ss, qs, i, peer).start()

    def arrive(own, inbox, ss, qs, n, peer):
        for i in range(1, n):
            message(own, inbox, ss, qs, i, peer).wait()

    barrier = pltpu.get_barrier_semaphore()
    for i in range(1, plane_n):
        pl.semaphore_signal(barrier, inc=1, device_id=plane_peer(i), device_id_type=MESH)
    for i in range(1, col_n):
        pl.semaphore_signal(barrier, inc=1, device_id=col_peer(i), device_id_type=MESH)
    pl.semaphore_wait(barrier, plane_n + col_n - 2)

    ks = range(len(subs))
    for k in ks:
        for d in range(2):
            send(d, 0, k).start()
    for s in range(steps):
        for k in ks:
            for d in range(2):
                load(d, s, k).start()
        if s == 0:
            w_loads = []
            for m in range(2):
                w_loads.append(
                    pltpu.make_async_copy(
                        wts[m].at[pl.ds(pl.multiple_of(pos * quarter, 16), quarter), :],
                        wbs[m], w_sem.at[m],
                    )
                )
                w_loads[m].start()
    for m in range(2):
        cas[m][...] = jnp.zeros_like(cas[m])
        w_loads[m].wait()
        n_strip = 16

        def weight_strip(i, acc, m=m):
            x = wbs[m][pl.ds(pl.multiple_of(i * n_strip, n_strip), n_strip), :].astype(jnp.float32)
            return acc + lane_sums(x * x)

        acc = lax.fori_loop(0, quarter // n_strip, weight_strip, jnp.zeros((n_strip, LANES), jnp.float32))
        at = (2 + m) * LANES
        own_upd[:, at : at + LANES] = jnp.sum(acc, axis=0, keepdims=True)

    for s in range(steps):
        for k in ks:
            m, j = subs[k]
            n = half // CUTS[m]
            for d in range(2):
                send(d, s, k).wait_recv()
                load(d, s, k).wait()

                def add_strip(i, carry, m=m, j=j, d=d, s=s, n=n):
                    at = pl.multiple_of(j * n + i * STRIP, STRIP)
                    x = rbs[m][d, s, pl.ds(at, STRIP), :] + lbs[m][d, s, pl.ds(at, STRIP), :]
                    rbs[m][d, s, pl.ds(at, STRIP), :] = x
                    if s == steps - 1:
                        square = x * x + 1e-30
                        rps[m][pl.ds(pl.multiple_of(d * half + at, STRIP), STRIP), :] = lane_sums(square)
                        cas[m][...] += square
                    return carry

                lax.fori_loop(0, n // STRIP, add_strip, 0)
                send(d, s + 1, k).start()
                if s == steps - 1:
                    keep(d, k).start()

    for m in range(2):
        to_lanes(rps[m], own_row, m * quarter)
        at = m * widths[0]
        own_col[:, at : at + widths[m]] = jnp.sum(cas[m][...], axis=0, keepdims=True)
    exchange(own_row, row_msg, s_row, q_row, col_n, col_peer)
    exchange(own_col, col_msg, s_col, q_col, plane_n, plane_peer)

    def forward(t):
        for k in ks:
            for d in range(2):
                send(d, steps + t, k).wait_recv()
                if t < steps - 1:
                    send(d, steps + t + 1, k).start()

    forward(0)
    arrive(own_row, row_msg, s_row, q_row, col_n, col_peer)
    arrive(own_col, col_msg, s_col, q_col, plane_n, plane_peer)
    decay = decay_ref[0]
    rest = 1.0 - decay
    row_tot, col_tot = own_row[...], own_col[...]
    for i in range(1, col_n):
        row_tot = row_tot + row_msg[i]
    for i in range(1, plane_n):
        col_tot = col_tot + col_msg[i]
    for m in range(2):
        row_new = decay * olds[m][pos] + rest * (
            row_tot[:, m * quarter : (m + 1) * quarter] / (widths[m] * col_n)
        )
        at = m * widths[0]
        col_new = decay * cols[m][...] + rest * (col_tot[:, at : at + widths[m]] / (tile * row_n))
        own_end[:, m * quarter : (m + 1) * quarter] = row_new
        cns[m][...] = col_new
        ics[m][...] = jnp.broadcast_to(1.0 / col_new, ics[m].shape)
        for d in range(2):

            def update_strip(i, carry, m=m, d=d):
                at = pl.multiple_of(i * STRIP, STRIP)
                x = rbs[m][d, steps - 1, pl.ds(at, STRIP), :]
                rps[m][pl.ds(pl.multiple_of(d * half + at, STRIP), STRIP), :] = lane_sums(x * x * ics[m][...])
                return carry

            lax.fori_loop(0, half // STRIP, update_strip, 0)
        to_lanes(rps[m], own_row, m * quarter)
        ratio = own_row[:, m * quarter : (m + 1) * quarter] / row_new
        own_upd[:, m * LANES : (m + 1) * LANES] = lane_sums(ratio)
    exchange(own_upd, upd_msg, s_upd, q_upd, col_n, col_peer)
    forward(1)
    arrive(own_upd, upd_msg, s_upd, q_upd, col_n, col_peer)
    upd = own_upd[...]
    for i in range(1, col_n):
        upd = upd + upd_msg[i]
    own_end[:, 2 * quarter :] = upd
    exchange(own_end, end_msg, s_end, q_end, plane_n, plane_peer)
    for t in range(2, steps):
        forward(t)
    arrive(own_end, end_msg, s_end, q_end, plane_n, plane_peer)
    end = own_end[...]
    for i in range(1, plane_n):
        end = end + end_msg[i]
    tot[...] = end
    for m in range(2):
        rns[m][pos] = own_end[:, m * quarter : (m + 1) * quarter]
        for b in range(1, dp_n):
            rns[m][(pos + dp_n - b) % dp_n] = end_msg[b * row_n, :, m * quarter : (m + 1) * quarter]
    for k in ks:
        for d in range(2):
            keep(d, k).wait()
            for s in range(2 * steps):
                send(d, s, k).wait_send()


def gather_sum(sizes, decay, grads, weights, rows, cols):
    dp_n, row_n, col_n = sizes
    tile = grads[0].shape[0]
    widths = tuple(g.shape[1] for g in grads)
    quarter, half = tile // dp_n, tile // (2 * dp_n)
    plane_n, steps, pieces = dp_n * row_n, dp_n - 1, sum(CUTS)
    f32 = jnp.float32
    shape = jax.ShapeDtypeStruct
    hbm = pl.BlockSpec(memory_space=pltpu.HBM)
    vmem = pl.BlockSpec(memory_space=pltpu.VMEM)
    smem = pl.BlockSpec(memory_space=pltpu.SMEM)
    dma = pltpu.SemaphoreType.DMA
    n_end = 2 * quarter + 4 * LANES
    scratch = [pltpu.VMEM((2, steps, half, n), f32) for n in widths] * 2
    scratch += [pltpu.VMEM((quarter, n), jnp.bfloat16) for n in widths]
    scratch += [pltpu.VMEM((STRIP, n), f32) for n in widths]
    scratch += [pltpu.VMEM((quarter, LANES), f32) for n in widths]
    scratch += [pltpu.VMEM((STRIP, n), f32) for n in widths]
    boxes = ((col_n, 2 * quarter), (plane_n, sum(widths)), (col_n, 4 * LANES), (plane_n, n_end))
    scratch += [pltpu.VMEM((n, 1, size), f32) for n, size in boxes]
    scratch += [pltpu.VMEM((1, size), f32) for n, size in boxes]
    scratch += [dma((2, 2 * steps, pieces)), dma((2, 2 * steps, pieces))]
    scratch += [dma((2, steps, pieces)), dma((2, pieces)), dma((2,))]
    for n, size in boxes:
        scratch += [dma((n,)), dma((n,))]
    return pl.pallas_call(
        functools.partial(kernel, sizes),
        out_shape=[shape((tile, n), f32) for n in widths]
        + [shape((dp_n, 1, quarter), f32)] * 2
        + [shape((1, n), f32) for n in widths]
        + [shape((1, n_end), f32)],
        in_specs=[smem] + [hbm] * 4 + [vmem] * 4,
        out_specs=[hbm] * 2 + [vmem] * 5,
        scratch_shapes=scratch,
        compiler_params=pltpu.CompilerParams(
            collective_id=0, has_side_effects=True, vmem_limit_bytes=58 * 2**20
        ),
    )(
        decay, *grads, *weights,
        *(r.reshape(dp_n, 1, quarter) for r in rows),
        *(c.reshape(1, -1) for c in cols),
    )


def body(
    sizes,
    step_count,
    ffn_weight, ffn_grads, ffn_rows, ffn_cols,
    attn_weight, attn_grads, attn_rows, attn_cols,
):
    dp_n, row_n, col_n = sizes
    decay = 1.0 - step_count.astype(jnp.float32) ** (-0.8)
    weights = (ffn_weight, attn_weight)
    full1, full2, rn1, rn2, cn1, cn2, tot = gather_sum(
        sizes, decay, (ffn_grads[0], attn_grads[0]), weights,
        (ffn_rows, attn_rows), (ffn_cols, attn_cols),
    )
    quarter = ffn_weight.shape[0] // dp_n
    tot = tot[0]
    outs = []
    for m, (full, rn, cn) in enumerate(((full1, rn1, cn1), (full2, rn2, cn2))):
        high = weights[m].shape[0] * row_n
        wide = weights[m].shape[1] * col_n
        entries = high * wide
        mean = jnp.sum(tot[m * quarter : (m + 1) * quarter]) / high
        at = 2 * quarter + m * LANES
        update_rms = jnp.sqrt(mean * jnp.sum(tot[at : at + LANES]) / entries)
        at += 2 * LANES
        factor = 0.01 * jnp.sqrt(jnp.sum(tot[at : at + LANES]) / entries)
        rows_new, cols_new = rn.reshape(-1), cn.reshape(-1)
        second = rows_new[:, None] * cols_new[None, :] / mean
        update = full / jnp.sqrt(second) / jnp.maximum(1.0, update_rms)
        fresh = weights[m].astype(jnp.float32) - factor * update
        outs += [fresh, update, rows_new, cols_new]
    return tuple(outs)


def solution(mesh):
    sizes = (mesh.shape["dp"], mesh.shape["row"], mesh.shape["col"])
    tiles = P("row", "col")
    grads = P("dp", "row", "col")
    one = (tiles, grads, P("row"), P("col"))
    result = (tiles, tiles, P("row"), P("col"))
    return jax.shard_map(
        functools.partial(body, sizes),
        mesh=mesh,
        in_specs=(P(), *one, *one),
        out_specs=(*result, *result),
        check_vma=False,
    )
```

time: 610 us -> 533 us (0.87)
  Pallas kernels: 0 us -> 485 us
  waiting for transfers between devices: 423 us -> 0 us
  blocking collectives: 109 us -> 0 us
  other arithmetic: 58.7 us -> 38.7 us
  between operations: 18.7 us -> 5.46 us
    pallas_call x0 -> x1, Pallas kernels: none -> 485 us  [gather_sum(): pl.pallas_call(functools.partial(kernel, sizes), out_shape=[shape((tile,...]
    reduce_scatter x2 -> x0, waiting for transfers between devices: 283 us -> none  [the longest x1 191 us: body(): lax.psum_scatter(ffn_grads[0], 'dp', scatter_dimension=0, tiled=True)]
    all_gather x2 -> x0, waiting for transfers between devices: 139 us -> none  [body(): lax.all_gather(g_part, 'dp', axis=0, tiled=True)]
    psum x5 -> x0, blocking collectives: 93.5 us -> none  [the longest x1 40.1 us: body(): update_tot = lax.psum((update_sq[0], update_sq[1]), ('dp', 'row', 'col'))]
    reduce_sum x7 -> x2, other arithmetic: 23.3 us -> 2.6 us  [the longest x1 1.31 us: body(): factor = 0.01 * jnp.sqrt(jnp.sum(tot[at:at + LANES]) / entries)]
    all_gather x2 -> x0, blocking collectives: 15.1 us -> none  [body(): row_full = lax.all_gather(row_sums, 'dp', axis=0, tiled=True)]
  transfers between devices with their start and end apart: 4 -> 0, of which waited for: 3 -> 0; matrix products, arithmetic and copies ran while one was open for 5% -> 0% of each run, Pallas kernels for 0% -> 0%
where the time goes in v2:
time: 533 us
  Pallas kernels  485 us (91%)
  other arithmetic  38.7 us (7%)
  between operations  5.46 us (1%)
    pallas_call x1, Pallas kernels, gather_sum(): pl.pallas_call(functools.partial(kernel, sizes), out_shape=[shape((tile,...  485 us
    sub x2, other arithmetic, body(): fresh = weights[m].astype(jnp.float32) - factor * update  35.4 us

profile of v2, /device:TPU:0, one launch (start us, length us, event | category | flops | bytes accessed | tf_op | source)
XLA Modules:
  0.0 532.6 jit_solution(15864144741893517253)
XLA Ops:
  1.3 1.3 reshape.42.c1
  2.6 485.4 %shard_map.152 = (f32[2048,2560]{1,0:T(8,128)}, f32[2048,1024]{1,0:T(8,128)}, f32[4,1,512]{2,1,0:T(1,128)}, f32[4,1,512]{2,1,0:T(1,128)}, f32[1,2560]{1,0:T(1,12...) custom-call(f32[1]{0:T(128)S(6)} %sub.9.decay_ref, f32[2048,2560]{1,0:T(8,128)} %bitcast.8, f32[2048,1024]{1,0:T(8,128)} %bitcast.9, ...), custom_call_target="tpu_custom_call" | custom-call | tf_op jit(solution)/shard_map/pallas_call | solution.py:285
  488.0 1.3 slice_reduce_fusion.3
  490.0 1.3 slice_reduce_fusion
  492.7 0.7 reduce.6
  493.4 0.0 copy-start
  493.4 0.0 copy-start.2
  493.4 0.0 copy-start.3
  493.4 25.4 %multiply_subtract_fusion = (f32[2048,2560]{1,0:T(8,128)}, f32[2048,2560]{1,0:T(8,128)}) fusion(bf16[2048,2560]{1,0:T(8,128)(2,1)} %w1.1, f32[]{:T(128)S(6)} %mul.58, f32[]{:T(128)S(6)} %max.6, f32[2048,2560]{1,0:T(8,128)} %get-tuple-element.16, f32[]{:T(128)S(6)} %div.49, f32[2560]{0:T(1024)S(1)} %reduce.6, f32[2048]{0:T(1024)} %bitcast.10), kind=kLoop, calls=%fused_computation | loop fusion | flops 36700160 | bytes 73418768 | tf_op jit(solution)/shard_map/sub | solution.py:332
  518.9 0.0 copy-done
  520.9 0.0 copy-done.2
  520.9 0.0 copy-done.3
  520.9 0.0 copy-start.1
  520.9 9.9 %multiply_subtract_fusion.1 = (f32[2048,1024]{1,0:T(8,128)}, f32[2048,1024]{1,0:T(8,128)}) fusion(bf16[2048,1024]{1,0:T(8,128)(2,1)} %w2.1, f32[]{:T(128)S(6)} %mul.67, f32[]{:T(128)S(6)} %max.7, f32[2048,1024]{1,0:T(8,128)} %get-tuple-element.19, f32[]{:T(128)S(6)} %div.57, f32[1024]{0:T(1024)S(1)} %bitcast.14, f32[2048]{0:T(1024)S(1)} %bitcast.12), kind=kLoop, calls=%fused_computation.2 | loop fusion | flops 14680064 | bytes 29372428 | tf_op jit(solution)/shard_map/sub | solution.py:332
  530.8 0.0 copy-done.1
  530.8 0.6 copy.21
  531.4 0.6 copy.22
  532.0 0.6 copy.23
Async XLA Ops:
  493.4 25.5 %copy-start = (f32[2560]{0:T(1024)}, f32[2560]{0:T(1024)S(1)}, u32[]{:S(2)}) copy-start(f32[2560]{0:T(1024)S(1)} %reduce.6) | copy-start | bytes 30724
  493.4 27.5 %copy-start.2 = (f32[4,1,512]{2,1,0:T(1,128)S(1)}, f32[4,1,512]{2,1,0:T(1,128)}, u32[]{:S(2)}) copy-start(f32[4,1,512]{2,1,0:T(1,128)} %get-tuple-element.20) | copy-start | bytes 24580
  493.4 27.5 %copy-start.3 = (f32[1,1024]{1,0:T(1,128)S(1)}, f32[1,1024]{1,0:T(1,128)}, u32[]{:S(2)}) copy-start(f32[1,1024]{1,0:T(1,128)} %get-tuple-element.21) | copy-start | bytes 12292
  520.9 9.9 %copy-start.1 = (f32[4,1,512]{2,1,0:T(1,128)S(1)}, f32[4,1,512]{2,1,0:T(1,128)}, u32[]{:S(2)}) copy-start(f32[4,1,512]{2,1,0:T(1,128)} %get-tuple-element.17) | copy-start | bytes 24580

commit v3 on v2

--- a/solution.py
+++ b/solution.py
@@ -11,6 +11,7 @@
 LANES = 128
 STRIP = 8
 CUTS = (4, 2)
+LATE = 1
 
 
 def gray(index):
@@ -57,6 +58,9 @@
     slot = pos * row_n + row
     subs = [(m, j) for m in range(2) for j in range(CUTS[m])]
 
+    def hops(k):
+        return 2 * steps - (subs[k][0] == LATE)
+
     def plane_peer(i):
         other = (slot + i) % plane_n
         return {"dp": gray(other // row_n), "row": other % row_n}
@@ -196,8 +200,9 @@
     def forward(t):
         for k in ks:
             for d in range(2):
-                send(d, steps + t, k).wait_recv()
-                if t < steps - 1:
+                if t < hops(k) - steps:
+                    send(d, steps + t, k).wait_recv()
+                if t + 1 < hops(k) - steps:
                     send(d, steps + t + 1, k).start()
 
     forward(0)
@@ -253,7 +258,7 @@
     for k in ks:
         for d in range(2):
             keep(d, k).wait()
-            for s in range(2 * steps):
+            for s in range(hops(k)):
                 send(d, s, k).wait_send()
 
 
@@ -301,6 +306,26 @@
     )
 
 
+def last_hop(full, dp_n):
+    pos = gray(lax.axis_index("dp"))
+    quarter, half = full.shape[0] // dp_n, full.shape[0] // (2 * dp_n)
+    ring = [gray(p) for p in range(dp_n)]
+    turns = ((0, 1), (1, dp_n - 1))
+    sent = []
+    for d, turn in turns:
+        at = (pos + turn * 2) % dp_n * quarter + d * half
+        sent.append(lax.dynamic_slice_in_dim(full, at, half, 0))
+    full, *sent = lax.optimization_barrier((full, *sent))
+    came = []
+    for d, turn in turns:
+        pairs = [(ring[p], ring[(p + turn) % dp_n]) for p in range(dp_n)]
+        came.append(lax.ppermute(sent[d], "dp", pairs))
+    for d, turn in turns:
+        at = (pos + turn) % dp_n * quarter + d * half
+        full = lax.dynamic_update_slice_in_dim(full, came[d], at, 0)
+    return full
+
+
 def body(
     sizes,
     step_count,
@@ -314,6 +339,7 @@
         sizes, decay, (ffn_grads[0], attn_grads[0]), weights,
         (ffn_rows, attn_rows), (ffn_cols, attn_cols),
     )
+    full2 = last_hop(full2, dp_n)
     quarter = ffn_weight.shape[0] // dp_n
     tot = tot[0]
     outs = []

time: 533 us -> 518 us (0.972)
  Pallas kernels: 485 us -> 463 us
    pallas_call x1, Pallas kernels: 485 us -> 463 us  [gather_sum(): pl.pallas_call(functools.partial(kernel, sizes), out_shape=[shape((tile,...]
  transfers between devices with their start and end apart: 0 -> 2, of which waited for: 0 -> 0; matrix products, arithmetic and copies ran while one was open for 0% -> 6% of each run, Pallas kernels for 0% -> 0%
where the time goes in v3:
time: 518 us; the launch traced here: 517 us
  Pallas kernels  463 us (89%)
  other arithmetic  38.7 us (7%)
  local copies, waits for them, and re-layouts  8.19 us (2%)
  between operations  5.51 us (1%)
    pallas_call x1, Pallas kernels, gather_sum(): pl.pallas_call(functools.partial(kernel, sizes), out_shape=[shape((tile,...  463 us
    sub x2, other arithmetic, body(): fresh = weights[m].astype(jnp.float32) - factor * update  35.4 us
  transfers between devices with their start and end apart: 2, of which 0 were waited for; matrix products, arithmetic and copies ran while one was open for 6% of the time, Pallas kernels for 0%

profile of v3, /device:TPU:0, one launch (start us, length us, event | category | flops | bytes accessed | tf_op | source)
XLA Modules:
  0.0 517.4 jit_solution(1178791655233494366)
XLA Ops:
  1.3 1.3 reshape.42.c1
  2.7 462.9 %shard_map.152 = (f32[2048,2560]{1,0:T(8,128)}, f32[2048,1024]{1,0:T(8,128)}, f32[4,1,512]{2,1,0:T(1,128)}, f32[4,1,512]{2,1,0:T(1,128)}, f32[1,2560]{1,0:T(1,12...) custom-call(f32[1]{0:T(128)S(6)} %sub.16.decay_ref, f32[2048,2560]{1,0:T(8,128)} %bitcast.8, f32[2048,1024]{1,0:T(8,128)} %bitcast.9, ...), custom_call_target="tpu_custom_call" | custom-call | tf_op jit(solution)/shard_map/pallas_call | solution.py:290
  465.6 1.7 constant_dynamic-slice_fusion
  467.3 0.6 collective-permute-start
  467.9 1.5 collective-permute-start.1
  469.4 1.3 slice_reduce_fusion.3
  470.7 1.3 slice_reduce_fusion
  474.0 0.7 reduce.6
  474.7 0.0 copy-start
  474.7 0.0 copy-start.2
  474.8 0.0 copy-start.3
  474.8 25.4 %multiply_subtract_fusion = (f32[2048,2560]{1,0:T(8,128)}, f32[2048,2560]{1,0:T(8,128)}) fusion(bf16[2048,2560]{1,0:T(8,128)(2,1)} %w1.1, f32[]{:T(128)S(6)} %mul.76, f32[]{:T(128)S(6)} %max.6, f32[2048,2560]{1,0:T(8,128)} %get-tuple-element.19, f32[]{:T(128)S(6)} %div.57, f32[2560]{0:T(1024)S(1)} %reduce.6, f32[2048]{0:T(1024)} %bitcast.10), kind=kLoop, calls=%fused_computation | loop fusion | flops 36700160 | bytes 73418768 | tf_op jit(solution)/shard_map/sub | solution.py:358
  500.2 0.0 copy-done
  502.2 0.0 collective-permute-done
  502.2 2.3 constant_dynamic-update-slice_fusion.1
  504.6 0.0 collective-permute-done.1
  504.6 1.0 constant_dynamic-update-slice_fusion
  505.6 0.0 copy-done.2
  505.6 0.0 copy-done.3
  505.6 0.0 copy-start.1
  505.6 9.9 %multiply_subtract_fusion.1 = (f32[2048,1024]{1,0:T(8,128)}, f32[2048,1024]{1,0:T(8,128)}) fusion(bf16[2048,1024]{1,0:T(8,128)(2,1)} %w2.1, f32[]{:T(128)S(6)} %mul.85, f32[]{:T(128)S(6)} %max.7, f32[2048,1024]{1,0:T(8,128)} %constant_dynamic-update-slice_fusion, f32[]{:T(128)S(6)} %div.68, f32[1024]{0:T(1024)S(1)} %bitcast.14, f32[2048]{0:T(1024)S(1)} %bitcast.12), kind=kLoop, calls=%fused_computation.2 | loop fusion | flops 14680064 | bytes 29372428 | tf_op jit(solution)/shard_map/sub | solution.py:358
  515.6 0.0 copy-done.1
  515.6 0.6 copy.23
  516.2 0.6 copy.24
  516.8 0.6 copy.25
Async XLA Ops:
  467.3 34.9 %collective-permute-start = (f32[256,1024]{1,0:T(8,128)S(1)}, f32[256,1024]{1,0:T(8,128)}, u32[]{:S(2)}, u32[]{:S(2)}) collective-permute-start(f32[256,1024]{1,0:T(8,128)S(1)} %get-tuple-element.24), channel_id=1, source_target_pairs={{0,8},{8,24},{24,16},{16,0},{1,9},{9,25},{25,17},{17,1},{2,10},{10... | collective-permute-start | bytes 3145736 | tf_op jit(solution)/shard_map/ppermute | solution.py:322
  467.9 36.7 %collective-permute-start.1 = (f32[256,1024]{1,0:T(8,128)S(1)}, f32[256,1024]{1,0:T(8,128)S(1)}, u32[]{:S(2)}, u32[]{:S(2)}) collective-permute-start(f32[256,1024]{1,0:T(8,128)S(1)} %get-tuple-element.25), channel_id=1, source_target_pairs={{0,16},{8,0},{24,8},{16,24},{1,17},{9,1},{25,9},{17,25},{2,18},{10... | collective-permute-start | bytes 3145736 | tf_op jit(solution)/shard_map/ppermute | solution.py:322
  474.7 25.5 %copy-start = (f32[2560]{0:T(1024)}, f32[2560]{0:T(1024)S(1)}, u32[]{:S(2)}) copy-start(f32[2560]{0:T(1024)S(1)} %reduce.6) | copy-start | bytes 30724
  474.7 30.9 %copy-start.2 = (f32[4,1,512]{2,1,0:T(1,128)S(1)}, f32[4,1,512]{2,1,0:T(1,128)}, u32[]{:S(2)}) copy-start(f32[4,1,512]{2,1,0:T(1,128)} %get-tuple-element.26) | copy-start | bytes 24580
  474.8 30.9 %copy-start.3 = (f32[1,1024]{1,0:T(1,128)S(1)}, f32[1,1024]{1,0:T(1,128)}, u32[]{:S(2)}) copy-start(f32[1,1024]{1,0:T(1,128)} %get-tuple-element.27) | copy-start | bytes 12292
  505.6 9.9 %copy-start.1 = (f32[4,1,512]{2,1,0:T(1,128)S(1)}, f32[4,1,512]{2,1,0:T(1,128)}, u32[]{:S(2)}) copy-start(f32[4,1,512]{2,1,0:T(1,128)} %get-tuple-element.20) | copy-start | bytes 24580

commit v4 on v3

--- a/solution.py
+++ b/solution.py
@@ -37,11 +37,11 @@
     sizes,
     decay_ref,
     g1, g2, w1, w2, r1, r2, c1, c2,
-    full1, full2, rn1, rn2, cn1, cn2, tot,
+    full1, full2, rn1, rn2, cn1, cn2, tot, late1, late2,
     rb1, rb2, lb1, lb2, wb1, wb2, ca1, ca2, rp1, rp2, ic1, ic2,
     row_msg, col_msg, upd_msg, end_msg,
     own_row, own_col, own_upd, own_end,
-    send_sem, recv_sem, load_sem, keep_sem, w_sem,
+    send_sem, recv_sem, load_sem, keep_sem, w_sem, late_sem,
     s_row, q_row, s_col, q_col, s_upd, q_upd, s_end, q_end,
 ):
     dp_n, row_n, col_n = sizes
@@ -93,6 +93,14 @@
             rbs[m].at[d, steps - 1, piece(m, j), :],
             fulls[m].at[place(m, j, d, pos), :],
             keep_sem.at[d, k],
+        )
+
+    def set_aside(d, k):
+        m, j = subs[k]
+        return pltpu.make_async_copy(
+            fulls[m].at[place(m, j, d, block(d, steps - 1)), :],
+            (late1, late2)[d].at[piece(m, j), :],
+            late_sem.at[d, k],
         )
 
     def send(d, s, k):
@@ -204,6 +212,8 @@
                     send(d, steps + t, k).wait_recv()
                 if t + 1 < hops(k) - steps:
                     send(d, steps + t + 1, k).start()
+                if subs[k][0] == LATE and t == steps - 2:
+                    set_aside(d, k).start()
 
     forward(0)
     arrive(own_row, row_msg, s_row, q_row, col_n, col_peer)
@@ -237,14 +247,13 @@
         ratio = own_row[:, m * quarter : (m + 1) * quarter] / row_new
         own_upd[:, m * LANES : (m + 1) * LANES] = lane_sums(ratio)
     exchange(own_upd, upd_msg, s_upd, q_upd, col_n, col_peer)
-    forward(1)
     arrive(own_upd, upd_msg, s_upd, q_upd, col_n, col_peer)
     upd = own_upd[...]
     for i in range(1, col_n):
         upd = upd + upd_msg[i]
     own_end[:, 2 * quarter :] = upd
     exchange(own_end, end_msg, s_end, q_end, plane_n, plane_peer)
-    for t in range(2, steps):
+    for t in range(1, steps):
         forward(t)
     arrive(own_end, end_msg, s_end, q_end, plane_n, plane_peer)
     end = own_end[...]
@@ -258,6 +267,8 @@
     for k in ks:
         for d in range(2):
             keep(d, k).wait()
+            if subs[k][0] == LATE:
+                set_aside(d, k).wait()
             for s in range(hops(k)):
                 send(d, s, k).wait_send()
 
@@ -284,7 +295,7 @@
     scratch += [pltpu.VMEM((n, 1, size), f32) for n, size in boxes]
     scratch += [pltpu.VMEM((1, size), f32) for n, size in boxes]
     scratch += [dma((2, 2 * steps, pieces)), dma((2, 2 * steps, pieces))]
-    scratch += [dma((2, steps, pieces)), dma((2, pieces)), dma((2,))]
+    scratch += [dma((2, steps, pieces)), dma((2, pieces)), dma((2,)), dma((2, pieces))]
     for n, size in boxes:
         scratch += [dma((n,)), dma((n,))]
     return pl.pallas_call(
@@ -292,9 +303,10 @@
         out_shape=[shape((tile, n), f32) for n in widths]
         + [shape((dp_n, 1, quarter), f32)] * 2
         + [shape((1, n), f32) for n in widths]
-        + [shape((1, n_end), f32)],
+        + [shape((1, n_end), f32)]
+        + [shape((half, widths[LATE]), f32)] * 2,
         in_specs=[smem] + [hbm] * 4 + [vmem] * 4,
-        out_specs=[hbm] * 2 + [vmem] * 5,
+        out_specs=[hbm] * 2 + [vmem] * 5 + [hbm] * 2,
         scratch_shapes=scratch,
         compiler_params=pltpu.CompilerParams(
             collective_id=0, has_side_effects=True, vmem_limit_bytes=58 * 2**20
@@ -306,16 +318,11 @@
     )
 
 
-def last_hop(full, dp_n):
+def last_hop(full, sent, dp_n):
     pos = gray(lax.axis_index("dp"))
     quarter, half = full.shape[0] // dp_n, full.shape[0] // (2 * dp_n)
     ring = [gray(p) for p in range(dp_n)]
     turns = ((0, 1), (1, dp_n - 1))
-    sent = []
-    for d, turn in turns:
-        at = (pos + turn * 2) % dp_n * quarter + d * half
-        sent.append(lax.dynamic_slice_in_dim(full, at, half, 0))
-    full, *sent = lax.optimization_barrier((full, *sent))
     came = []
     for d, turn in turns:
         pairs = [(ring[p], ring[(p + turn) % dp_n]) for p in range(dp_n)]
@@ -335,11 +342,11 @@
     dp_n, row_n, col_n = sizes
     decay = 1.0 - step_count.astype(jnp.float32) ** (-0.8)
     weights = (ffn_weight, attn_weight)
-    full1, full2, rn1, rn2, cn1, cn2, tot = gather_sum(
+    full1, full2, rn1, rn2, cn1, cn2, tot, *sent = gather_sum(
         sizes, decay, (ffn_grads[0], attn_grads[0]), weights,
         (ffn_rows, attn_rows), (ffn_cols, attn_cols),
     )
-    full2 = last_hop(full2, dp_n)
+    full2 = last_hop(full2, sent, dp_n)
     quarter = ffn_weight.shape[0] // dp_n
     tot = tot[0]
     outs = []

time: 518 us -> 514 us (level)
  no operation moved by 1% of the time
where the time goes in v4:
time: 514 us
  Pallas kernels  462 us (90%)
  other arithmetic  38.6 us (8%)
  between operations  5.47 us (1%)
  local copies, waits for them, and re-layouts  5.24 us (1%)
    pallas_call x1, Pallas kernels, gather_sum(): pl.pallas_call(functools.partial(kernel, sizes), out_shape=[shape((tile,...  462 us
    sub x2, other arithmetic, body(): fresh = weights[m].astype(jnp.float32) - factor * update  35.4 us
  transfers between devices with their start and end apart: 2, of which 0 were waited for; matrix products, arithmetic and copies ran while one was open for 6% of the time, Pallas kernels for 0%

profile of v4, /device:TPU:0, one launch (start us, length us, event | category | flops | bytes accessed | tf_op | source)
XLA Modules:
  0.0 513.7 jit_solution(7592185742072571043)
XLA Ops:
  1.3 1.3 reshape.42.c1
  2.6 462.3 %shard_map.152 = (f32[2048,2560]{1,0:T(8,128)}, f32[2048,1024]{1,0:T(8,128)}, f32[4,1,512]{2,1,0:T(1,128)}, f32[4,1,512]{2,1,0:T(1,128)}, f32[1,2560]{1,0:T(1,12...) custom-call(f32[1]{0:T(128)S(6)} %sub.16.decay_ref, ...), custom_call_target="tpu_custom_call" | custom-call | tf_op jit(solution)/shard_map/pallas_call | solution.py:301
  464.9 1.5 collective-permute-start
  466.5 0.5 collective-permute-start.1
  467.0 1.2 slice_reduce_fusion.3
  468.3 1.3 slice_reduce_fusion
  471.6 0.7 reduce.6
  472.3 0.0 copy-start
  472.3 0.0 copy-start.2
  472.3 0.0 copy-start.3
  472.4 25.4 %multiply_subtract_fusion = (f32[2048,2560]{1,0:T(8,128)}, f32[2048,2560]{1,0:T(8,128)}) fusion(bf16[2048,2560]{1,0:T(8,128)(2,1)} %w1.1, f32[]{:T(128)S(6)} %mul.70, f32[]{:T(128)S(6)} %max.6, f32[2048,2560]{1,0:T(8,128)} %get-tuple-element.18, f32[]{:T(128)S(6)} %div.57, f32[2560]{0:T(1024)S(1)} %reduce.6, f32[2048]{0:T(1024)} %bitcast.10), kind=kLoop, calls=%fused_computation | loop fusion | flops 36700160 | bytes 73418768 | tf_op jit(solution)/shard_map/sub | solution.py:365
  497.8 0.0 copy-done
  499.8 0.0 collective-permute-done
  499.8 1.1 constant_dynamic-update-slice_fusion.1
  500.9 0.0 collective-permute-done.1
  500.9 1.0 constant_dynamic-update-slice_fusion
  502.0 0.0 copy-done.2
  502.0 0.0 copy-done.3
  502.0 0.0 copy-start.1
  502.0 9.9 %multiply_subtract_fusion.1 = (f32[2048,1024]{1,0:T(8,128)}, f32[2048,1024]{1,0:T(8,128)}) fusion(bf16[2048,1024]{1,0:T(8,128)(2,1)} %w2.1, f32[]{:T(128)S(6)} %mul.79, f32[]{:T(128)S(6)} %max.7, f32[2048,1024]{1,0:T(8,128)} %constant_dynamic-update-slice_fusion, f32[]{:T(128)S(6)} %div.68, f32[1024]{0:T(1024)S(1)} %bitcast.14, f32[2048]{0:T(1024)S(1)} %bitcast.12), kind=kLoop, calls=%fused_computation.2 | loop fusion | flops 14680064 | bytes 29372428 | tf_op jit(solution)/shard_map/sub | solution.py:365
  511.9 0.0 copy-done.1
  511.9 0.6 copy.23
  512.5 0.6 copy.24
  513.1 0.6 copy.25
Async XLA Ops:
  464.9 34.9 %collective-permute-start = (f32[256,1024]{1,0:T(8,128)}, f32[256,1024]{1,0:T(8,128)S(1)}, u32[]{:S(2)}, u32[]{:S(2)}) collective-permute-start(f32[256,1024]{1,0:T(8,128)} %get-tuple-element.22), channel_id=1, source_target_pairs={{0,8},{8,24},{24,16},{16,0},{1,9},{9,25},{25,17},{17,1},{2,10},{10... | collective-permute-start | bytes 3145736 | tf_op jit(solution)/shard_map/ppermute | solution.py:329
  466.5 34.4 %collective-permute-start.1 = (f32[256,1024]{1,0:T(8,128)}, f32[256,1024]{1,0:T(8,128)S(1)}, u32[]{:S(2)}, u32[]{:S(2)}) collective-permute-start(f32[256,1024]{1,0:T(8,128)} %get-tuple-element.23), channel_id=1, source_target_pairs={{0,16},{8,0},{24,8},{16,24},{1,17},{9,1},{25,9},{17,25},{2,18},{10... | collective-permute-start | bytes 3145736 | tf_op jit(solution)/shard_map/ppermute | solution.py:329
  472.3 25.5 %copy-start = (f32[2560]{0:T(1024)}, f32[2560]{0:T(1024)S(1)}, u32[]{:S(2)}) copy-start(f32[2560]{0:T(1024)S(1)} %reduce.6) | copy-start | bytes 30724
  472.3 29.6 %copy-start.2 = (f32[4,1,512]{2,1,0:T(1,128)S(1)}, f32[4,1,512]{2,1,0:T(1,128)}, u32[]{:S(2)}) copy-start(f32[4,1,512]{2,1,0:T(1,128)} %get-tuple-element.24) | copy-start | bytes 24580
  472.3 29.6 %copy-start.3 = (f32[1,1024]{1,0:T(1,128)S(1)}, f32[1,1024]{1,0:T(1,128)}, u32[]{:S(2)}) copy-start(f32[1,1024]{1,0:T(1,128)} %get-tuple-element.25) | copy-start | bytes 12292
  502.0 9.9 %copy-start.1 = (f32[4,1,512]{2,1,0:T(1,128)S(1)}, f32[4,1,512]{2,1,0:T(1,128)}, u32[]{:S(2)}) copy-start(f32[4,1,512]{2,1,0:T(1,128)} %get-tuple-element.19) | copy-start | bytes 24580
